TPU v7x, 32 devices: a whole 2x2x4 slice. The times are simulated.
32 devices in a mesh: frame: 4 (over y, core), tensor: 8 (over z, x).
Axes of the slice: x: 2, y: 2, z: 4, core: 2. Of those that a mesh axis runs over, the one named last changes fastest.
Arguments:
- latent: bfloat16 [7680, 1152], P('frame', 'tensor'), may hold values from -6 to 6
- timestep: int32 [1], replicated, may hold values from 0 to 999
- frame_pos: int32 [4], P('frame'), may hold values from 0 to 4095
- time_w1: bfloat16 [256, 1152], replicated, may hold values from -0.375 to 0.375
- time_w2: bfloat16 [1152, 1152], P(None, 'tensor'), may hold values from -0.1875 to 0.1875
- ada_w: bfloat16 [1152, 10368], P('tensor'), may hold values from -0.1875 to 0.1875
- w_sqkv: bfloat16 [1152, 3456], P(None, 'tensor'), may hold values from -0.70710678 to 0.70710678
- w_so: bfloat16 [1152, 1152], P('tensor'), may hold values from -0.25 to 0.25
- w_tqkv: bfloat16 [1152, 3456], P(None, 'tensor'), may hold values from -0.70710678 to 0.70710678
- w_to: bfloat16 [1152, 1152], P('tensor'), may hold values from -0.25 to 0.25
- w_fc1: bfloat16 [1152, 4608], P(None, 'tensor'), may hold values from -0.1875 to 0.1875
- w_fc2: bfloat16 [4608, 1152], P('tensor'), may hold values from -0.125 to 0.125
Outputs:
- block_out: bfloat16 [7680, 1152], P('frame', 'tensor')
All inputs are finite; a program needn't handle non-finite values.
Results may differ from a plain program's by a relative error of at most 0.025.
Values may be sent and summed in bfloat16 or wider, within the bound.
A program may use at most 128 MiB of HBM per device.

v0:
```python
import math

import jax
import jax.numpy as jnp
from jax import lax
from jax.sharding import PartitionSpec as P

D = 1152
HD = 72
P_SIZE = 1920


def layer_norm(values_in):
    center = values_in - jnp.mean(values_in, axis=-1, keepdims=True)
    spread = jnp.mean(center * center, axis=-1, keepdims=True)
    return center * lax.rsqrt(spread + 1e-06)


def branch_input(stream, shift, scale):
    return (layer_norm(stream.astype(jnp.float32)) * (1.0 + scale) + shift).astype(jnp.bfloat16)


def time_features(timestep, width):
    half_width = width // 2
    frequency = jnp.exp(-math.log(10000.0) * jnp.arange(half_width, dtype=jnp.float32) / half_width)
    angles = timestep.astype(jnp.float32)[:, None] * frequency[None, :]
    return jnp.concatenate([jnp.cos(angles), jnp.sin(angles)], axis=1).astype(jnp.bfloat16)


def rotate(projected, positions):
    half_width = HD // 2
    frequency = jnp.exp(-math.log(10000.0) * jnp.arange(half_width, dtype=jnp.float32) / half_width)
    angles = positions.astype(jnp.float32)[:, None] * frequency[None, :]
    cosine = jnp.cos(angles)[:, None, None, :]
    sine_part = jnp.sin(angles)[:, None, None, :]

    def turn(section):
        section = section.astype(jnp.float32)
        first_half = section[..., :half_width]
        second_half = section[..., half_width:]
        turned = jnp.concatenate(
            [
                first_half * cosine - second_half * sine_part,
                first_half * sine_part + second_half * cosine,
            ],
            axis=-1,
        )
        return turned.astype(jnp.bfloat16)

    return jnp.stack(
        [turn(projected[:, :, :, 0]), turn(projected[:, :, :, 1]), projected[:, :, :, 2]], axis=3
    )


def spatial_branch(normed, w_qkv, w_out):
    row_count = normed.shape[0]
    heads_local = w_out.shape[0] // HD
    projected = jnp.dot(normed, w_qkv, preferred_element_type=jnp.float32).astype(jnp.bfloat16)
    projected = projected.reshape(row_count // P_SIZE, P_SIZE, heads_local, 3, HD)
    scores = jnp.einsum(
        "fphd,fqhd->fhpq",
        projected[:, :, :, 0],
        projected[:, :, :, 1],
        preferred_element_type=jnp.float32,
    ) * HD ** (-0.5)
    weights = jax.nn.softmax(scores, axis=-1).astype(jnp.bfloat16)
    attended = jnp.einsum(
        "fhpq,fqhd->fphd", weights, projected[:, :, :, 2], preferred_element_type=jnp.float32
    ).astype(jnp.bfloat16)
    return jnp.dot(
        attended.reshape(row_count, heads_local * HD), w_out, preferred_element_type=jnp.float32
    )


def temporal_branch(normed, w_qkv, w_out, frame_pos):
    row_count = normed.shape[0]
    heads_local = w_out.shape[0] // HD
    frames_local = row_count // P_SIZE
    projected = jnp.dot(normed, w_qkv, preferred_element_type=jnp.float32).astype(jnp.bfloat16)
    projected = projected.reshape(frames_local, P_SIZE, heads_local, 3, HD)
    rotated = rotate(projected, frame_pos).reshape(frames_local, P_SIZE, heads_local, 3 * HD)
    head_block = lax.all_to_all(rotated, "frame", split_axis=1, concat_axis=0, tiled=True)
    frame_count = head_block.shape[0]
    position_count = head_block.shape[1]
    head_count = head_block.shape[2]
    split_parts = head_block.reshape(frame_count, position_count, head_count, 3, HD)
    scores = jnp.einsum(
        "fphd,gphd->phfg",
        split_parts[:, :, :, 0],
        split_parts[:, :, :, 1],
        preferred_element_type=jnp.float32,
    ) * HD ** (-0.5)
    weights = jax.nn.softmax(scores, axis=-1).astype(jnp.bfloat16)
    by_position = jnp.einsum(
        "phfg,gphd->fphd", weights, split_parts[:, :, :, 2], preferred_element_type=jnp.float32
    ).astype(jnp.bfloat16)
    by_frame = lax.all_to_all(by_position, "frame", split_axis=0, concat_axis=1, tiled=True)
    return jnp.dot(
        by_frame.reshape(row_count, heads_local * HD), w_out, preferred_element_type=jnp.float32
    )


def mlp_branch(normed, w_fc1, w_fc2):
    mlp_hidden = jax.nn.gelu(
        jnp.dot(normed, w_fc1, preferred_element_type=jnp.float32), approximate=True
    ).astype(jnp.bfloat16)
    return jnp.dot(mlp_hidden, w_fc2, preferred_element_type=jnp.float32)


def shards(
    latent, timestep, frame_pos, time_w1, time_w2, ada_w, w_sqkv, w_so, w_tqkv, w_to, w_fc1, w_fc2
):
    time_embed = time_features(timestep, time_w1.shape[0])
    hidden_time = jax.nn.silu(
        jnp.dot(time_embed, time_w1, preferred_element_type=jnp.float32)
    ).astype(jnp.bfloat16)
    condition = jax.nn.silu(
        jnp.dot(hidden_time, time_w2, preferred_element_type=jnp.float32)
    ).astype(jnp.bfloat16)
    partial_mod = jnp.dot(condition, ada_w, preferred_element_type=jnp.float32)
    modulation = lax.psum(partial_mod.astype(jnp.bfloat16), "tensor").astype(jnp.float32)[0]
    own_width = latent.shape[1]
    tensor_index = lax.axis_index("tensor")

    def mod_vector(index):
        return modulation[index * D : (index + 1) * D]

    def run_branch(segment_index, normed):
        if segment_index == 0:
            return spatial_branch(normed, w_sqkv, w_so)
        if segment_index == 1:
            return temporal_branch(normed, w_tqkv, w_to, frame_pos)
        return mlp_branch(normed, w_fc1, w_fc2)

    own_block = latent
    for segment_index in range(3):
        full_rows = lax.all_gather(own_block, "tensor", axis=1, tiled=True)
        normed = branch_input(
            full_rows, mod_vector(3 * segment_index), mod_vector(3 * segment_index + 1)
        )
        partial_terms = run_branch(segment_index, normed)
        summed = lax.psum_scatter(
            partial_terms.astype(jnp.bfloat16), "tensor", scatter_dimension=1, tiled=True
        ).astype(jnp.float32)
        own_block = (
            own_block.astype(jnp.float32)
            + lax.dynamic_slice_in_dim(
                mod_vector(3 * segment_index + 2), tensor_index * own_width, own_width, 0
            )
            * summed
        ).astype(jnp.bfloat16)
    return own_block


def solution(mesh):
    placed = (
        P("frame", "tensor"),
        P(),
        P("frame"),
        P(),
        P(None, "tensor"),
        P("tensor", None),
        P(None, "tensor"),
        P("tensor", None),
        P(None, "tensor"),
        P("tensor", None),
        P(None, "tensor"),
        P("tensor", None),
    )
    return jax.shard_map(
        shards, mesh=mesh, in_specs=placed, out_specs=P("frame", "tensor"), check_vma=False
    )
```

profile of v0, /device:TPU:0, one launch (start us, length us, event | category | flops | bytes accessed | tf_op | source)
XLA Modules:
  0.0 669.7 jit_solution(9377820953988734554)
XLA Ops:
  11.3 40.3 %psum.7 = bf16[1,10368]{1,0:T(2,128)(2,1)S(1)} all-reduce(bf16[1,10368]{1,0:T(2,128)(2,1)S(1)} %convert_element_type.165), channel_id=1, replica_groups=mesh['frame'=4,'tensor'=8] {'tensor'}, use_global_device_ids=true, to_apply=%region_0.1 | all-reduce | flops 10368 | bytes 41472 | tf_op jit(solution)/shard_map/psum | solution.py:121
  51.7 37.8 %all-gather.4.cloned.1.call-done = bf16[1920,1152]{0,1:T(8,128)(2,1)} async-done(((bf16[1920,144]{0,1:T(8,128)(2,1)}), bf16[1920,1152]{0,1:T(8,128)(2,1)}) %all-gather.4.cloned.1.call-update) | async-done | bytes 4423696 | tf_op jit(solution)/shard_map/all_gather | solution.py:137
  89.4 3.1 convert_reduce_fusion.2
  94.2 3.9 fusion.56
  98.1 15.2 %fusion.89 = (f32[2,1920]{1,0:T(2,128)S(1)}, f32[2,1920,1920]{1,2,0:T(8,128)}) fusion(bf16[1,1920,2,3,72]{1,4,3,2,0:T(8,128)(2,1)} %bitcast.113), kind=kOutput, calls=%fused_computation.134 | convolution fusion | flops 1083803520 | bytes 30612480 | tf_op jit(solution)/shard_map/sub | solution.py:66
  113.3 12.2 %fusion.61 = bf16[2,72,1920]{2,1,0:T(8,128)(2,1)S(1)} fusion(f32[2,1920,1920]{1,2,0:T(8,128)} %get-tuple-element.27, f32[2,1920]{1,0:T(2,128)S(1)} %get-tuple-element.26, bf16[1,1920,2,3,72]{1,4,3,2,0:T(8,128)(2,1)} %bitcast.114), kind=kOutput, calls=%fused_computation.62 | convolution fusion | flops 1076705280 | bytes 30612480 | tf_op jit(solution)/shard_map/fhpq,fqhd->fphd/dot_general | solution.py:67
  125.5 3.5 convolution_convert_fusion.2
  129.2 88.7 %reduce-scatter.4.cloned.1.call-done = bf16[1920,144]{0,1:T(8,128)(2,1)} async-done(((bf16[1920,1152]{0,1:T(8,128)(2,1)}), bf16[1920,144]{0,1:T(8,128)(2,1)}) %reduce-scatter.4.cloned.1.call-update) | async-done | bytes 552976 | tf_op jit(solution)/shard_map/reduce_scatter | solution.py:142
  220.8 75.7 %all-gather.6.cloned.1.call-done = bf16[1920,1152]{0,1:T(8,128)(2,1)} async-done(((bf16[1920,144]{0,1:T(8,128)(2,1)}), bf16[1920,1152]{0,1:T(8,128)(2,1)}) %all-gather.6.cloned.1.call-update) | async-done | bytes 4423696 | tf_op jit(solution)/shard_map/all_gather | solution.py:137
  296.4 3.1 convert_reduce_fusion.1
  301.2 2.7 fusion.53
  306.2 5.2 copy.58
  311.4 27.7 %all_to_all.8 = bf16[1,1920,2,216]{3,2,0,1:T(2,128)(2,1)} all-to-all(bf16[1,1920,2,216]{3,2,0,1:T(2,128)(2,1)S(1)} %copy.58), channel_id=1, replica_groups=mesh['frame'=4,'tensor'=8] {'frame'}, dimensions={1} | all-to-all | bytes 3317760 | tf_op jit(solution)/shard_map/all_to_all | solution.py:82
  339.1 9.5 %reshape.299 = bf16[4,480,2,3,72]{4,3,2,1,0:T(4,128)(2,1)} reshape(bf16[1,1920,2,216]{3,2,0,1:T(2,128)(2,1)} %all_to_all.8) | data formatting | bytes 3317760 | tf_op jit(solution)/shard_map/reshape | solution.py:86
  348.6 10.4 %fusion.87 = (bf16[4,480,2,1,72]{4,3,2,1,0:T(2,128)(2,1)}, bf16[4,480,2,1,72]{4,3,2,1,0:T(2,128)(2,1)S(1)}, bf16[4,480,2,1,72]{4,3,2,1,0:T(2,128)(2,1)}) fusion(bf16[4,480,2,3,72]{4,3,2,1,0:T(4,128)(2,1)} %reshape.299), kind=kLoop, calls=%fused_computation.132 | loop fusion | bytes 3317760 | tf_op jit(solution)/shard_map/slice | solution.py:89
  359.0 8.6 %fusion.90 = (f32[480,2,4]{2,1,0:T(2,128)}, f32[480,2,4,4]{2,3,1,0:T(4,128)}) fusion(bf16[4,480,2,1,72]{4,3,2,1,0:T(2,128)(2,1)} %get-tuple-element.13, bf16[4,480,2,1,72]{4,3,2,1,0:T(2,128)(2,1)} %get-tuple-element.11), kind=kOutput, calls=%fused_computation.135 | convolution fusion | flops 2257923 | bytes 1182720 | tf_op jit(solution)/shard_map/sub | solution.py:93
  367.6 3.5 fusion.63
  372.0 11.9 %all_to_all.9 = bf16[4,480,2,72]{1,3,2,0:T(8,128)(2,1)S(1)} all-to-all(bf16[4,480,2,72]{1,3,2,0:T(8,128)(2,1)S(1)} %copy.64), channel_id=1, replica_groups=mesh['frame'=4,'tensor'=8] {'frame'}, dimensions={0} | all-to-all | bytes 1105920 | tf_op jit(solution)/shard_map/all_to_all | solution.py:97
  385.1 3.5 convolution_convert_fusion.1
  388.8 87.8 %reduce-scatter.6.cloned.1.call-done = bf16[1920,144]{0,1:T(8,128)(2,1)} async-done(((bf16[1920,1152]{0,1:T(8,128)(2,1)}), bf16[1920,144]{0,1:T(8,128)(2,1)}) %reduce-scatter.6.cloned.1.call-update) | async-done | bytes 552976 | tf_op jit(solution)/shard_map/reduce_scatter | solution.py:142
  479.0 75.9 %all-gather.8.cloned.1.call-done = bf16[1920,1152]{0,1:T(8,128)(2,1)} async-done(((bf16[1920,144]{0,1:T(8,128)(2,1)}), bf16[1920,1152]{0,1:T(8,128)(2,1)}) %all-gather.8.cloned.1.call-update) | async-done | bytes 4423696 | tf_op jit(solution)/shard_map/all_gather | solution.py:137
  555.0 3.1 convert_reduce_fusion
  559.8 11.7 %convolution_convert_fusion = bf16[1920,1152]{0,1:T(8,128)(2,1)} fusion(bf16[576,1152]{1,0:T(8,128)(2,1)} %param.23, bf16[1152,576]{0,1:T(8,128)(2,1)} %param.22, bf16[1920,1152]{0,1:T(8,128)(2,1)} %all-gather.8.cloned.1.call-done, f32[1152]{0:T(1024)S(1)} %get-tuple-element.6, f32[1152]{0:T(1024)S(1)} %get-tuple-element.5, f32[1920]{0:T(1024)S(1)} %add_rsqrt_fusion, ...), kind=kOutput, calls=%fused_computation.32 | convolution fusion | flops 5121515520 | bytes 11526144 | tf_op jit(solution)/shard_map/dot_general | solution.py:107
  571.6 88.7 %reduce-scatter.8.cloned.1.call-done = bf16[1920,144]{0,1:T(8,128)(2,1)} async-done(((bf16[1920,1152]{0,1:T(8,128)(2,1)}), bf16[1920,144]{0,1:T(8,128)(2,1)}) %reduce-scatter.8.cloned.1.call-update) | async-done | bytes 552976 | tf_op jit(solution)/shard_map/reduce_scatter | solution.py:142
  (74 shorter events, 20.5 us)
Async XLA Ops:
  6.5 4.2 copy-start
  6.5 82.9 %all-gather.4.cloned.1.call-start = ((), (), s32[]{:S(2)}) async-start(), calls=%async_computation.5 | async-start | bytes 4976640 | tf_op jit(solution)/shard_map/all_gather | solution.py:137
  7.3 210.6 %reduce-scatter.4.cloned.1.call-start = ((), (), s32[]{:S(2)}) async-start(), calls=%async_computation.6 | async-start | bytes 4976640 | tf_op jit(solution)/shard_map/reduce_scatter | solution.py:142
  89.4 3.6 copy-start.2
  89.4 4.8 copy-start.10
  113.3 12.2 %copy-start.8 = (bf16[144,1152]{1,0:T(8,128)(2,1)S(1)}, bf16[144,1152]{1,0:T(8,128)(2,1)}, u32[]{:S(2)}) copy-start(bf16[144,1152]{1,0:T(8,128)(2,1)} %param.19) | copy-start | bytes 995332
  125.5 92.4 %copy-start.7 = (bf16[1920,144]{0,1:T(8,128)(2,1)S(1)}, bf16[1920,144]{0,1:T(8,128)(2,1)}, u32[]{:S(2)}) copy-start(bf16[1920,144]{0,1:T(8,128)(2,1)} %param.12) | copy-start | bytes 1658884
  129.1 167.4 %all-gather.6.cloned.1.call-start = ((), (), s32[]{:S(2)}) async-start(), calls=%async_computation.7 | async-start | bytes 4976640 | tf_op jit(solution)/shard_map/all_gather | solution.py:137
  220.0 256.6 %reduce-scatter.6.cloned.1.call-start = ((), (), s32[]{:S(2)}) async-start(), calls=%async_computation.8 | async-start | bytes 4976640 | tf_op jit(solution)/shard_map/reduce_scatter | solution.py:142
  296.4 3.6 copy-start.3
  296.4 4.8 copy-start.11
  371.1 14.0 %copy-start.9 = (bf16[144,1152]{1,0:T(8,128)(2,1)S(1)}, bf16[144,1152]{1,0:T(8,128)(2,1)}, u32[]{:S(2)}) copy-start(bf16[144,1152]{1,0:T(8,128)(2,1)} %param.21) | copy-start | bytes 995332
  385.1 91.5 %copy-start.5 = (bf16[1920,144]{0,1:T(8,128)(2,1)S(1)}, bf16[1920,144]{0,1:T(8,128)(2,1)}, u32[]{:S(2)}) copy-start(bf16[1920,144]{0,1:T(8,128)(2,1)} %add_convert_fusion.2) | copy-start | bytes 1658884
  388.7 166.3 %all-gather.8.cloned.1.call-start = ((), (), s32[]{:S(2)}) async-start(), calls=%async_computation.9 | async-start | bytes 4976640 | tf_op jit(solution)/shard_map/all_gather | solution.py:137
  478.7 181.6 %reduce-scatter.8.cloned.1.call-start = ((), (), s32[]{:S(2)}) async-start(), calls=%async_computation.10 | async-start | bytes 4976640 | tf_op jit(solution)/shard_map/reduce_scatter | solution.py:142
  555.0 3.6 copy-start.4
  559.8 102.6 %copy-start.1 = (bf16[144,10368]{1,0:T(8,128)(2,1)S(1)}, bf16[144,10368]{1,0:T(8,128)(2,1)}, u32[]{:S(2)}) copy-start(bf16[144,10368]{1,0:T(8,128)(2,1)} %param.17) | copy-start | bytes 8957956
  571.5 88.8 %copy-start.6 = (bf16[1920,144]{0,1:T(8,128)(2,1)S(1)}, bf16[1920,144]{0,1:T(8,128)(2,1)}, u32[]{:S(2)}) copy-start(bf16[1920,144]{0,1:T(8,128)(2,1)} %add_convert_fusion.1) | copy-start | bytes 1658884
Sparse Core Ops, SparseCore 0:
  9.5 79.8 all-gather.3
  129.2 88.6 reduce-scatter.3
  220.3 76.0 all-gather.5
  388.8 87.7 reduce-scatter.5
  478.9 76.0 all-gather.7
  571.7 88.6 reduce-scatter.7
where the time goes:
time: 678 us; the launch traced here: 670 us
  waiting for transfers between devices  455 us (67%)
  blocking collectives  79.9 us (12%)
  matrix products  67.7 us (10%)
  local copies, waits for them, and re-layouts  29 us (4%)
  other arithmetic  21.7 us (3%)
  between operations  15.6 us (2%)
    reduce_scatter x3, waiting for transfers between devices, shards(): lax.psum_scatter(partial_terms.astype(jnp.bfloat16), 'tensor', scatter_di...  265 us
    all_gather x3, waiting for transfers between devices, shards(): full_rows = lax.all_gather(own_block, 'tensor', axis=1, tiled=True)  189 us
    psum x1, blocking collectives, shards(): lax.psum(partial_mod.astype(jnp.bfloat16), 'tensor').astype(jnp.float32)[0]  40.3 us
    all_to_all x1, blocking collectives, temporal_branch(): lax.all_to_all(rotated, 'frame', split_axis=1, concat_axis=0, tiled=True)  27.7 us
    sub x1, matrix products, spatial_branch(): weights = jax.nn.softmax(scores, axis=-1).astype(jnp.bfloat16)  15.2 us
  transfers between devices with their start and end apart: 6, of which 6 were waited for; matrix products, arithmetic and copies ran while one was open for 1% of the time, Pallas kernels for 0%

commit v1 on v0

v1 whole, which is shorter than its diff:
```python
import math

import jax
import jax.numpy as jnp
from jax import lax
from jax.sharding import PartitionSpec as P

D = 1152
HD = 72
P_SIZE = 1920


def layer_norm(values_in):
    center = values_in - jnp.mean(values_in, axis=-1, keepdims=True)
    spread = jnp.mean(center * center, axis=-1, keepdims=True)
    return center * lax.rsqrt(spread + 1e-06)


def branch_input(stream, shift, scale):
    return (layer_norm(stream.astype(jnp.float32)) * (1.0 + scale) + shift).astype(jnp.bfloat16)


def time_features(timestep, width):
    half_width = width // 2
    frequency = jnp.exp(-math.log(10000.0) * jnp.arange(half_width, dtype=jnp.float32) / half_width)
    angles = timestep.astype(jnp.float32)[:, None] * frequency[None, :]
    return jnp.concatenate([jnp.cos(angles), jnp.sin(angles)], axis=1).astype(jnp.bfloat16)


def bdot(a, b):
    return jnp.dot(a, b, preferred_element_type=jnp.float32)


def spatial_attention(normed, w_qkv):
    heads_local = w_qkv.shape[1] // (3 * HD)
    projected = bdot(normed, w_qkv).astype(jnp.bfloat16)
    projected = projected.reshape(P_SIZE, heads_local, 3, HD)
    scores = jnp.einsum(
        "phd,qhd->hpq", projected[:, :, 0], projected[:, :, 1], preferred_element_type=jnp.float32
    ) * HD ** (-0.5)
    weights = jax.nn.softmax(scores, axis=-1).astype(jnp.bfloat16)
    attended = jnp.einsum(
        "hpq,qhd->phd", weights, projected[:, :, 2], preferred_element_type=jnp.float32
    ).astype(jnp.bfloat16)
    return attended.reshape(P_SIZE, heads_local * HD)


def gather_rows(shard, frame_count, frame_index):
    rows = shard.shape[0]
    if rows % frame_count:
        return lax.all_gather(shard, "tensor", axis=0, tiled=True)
    part = rows // frame_count
    mine = lax.dynamic_slice_in_dim(shard, frame_index * part, part, 0)
    return lax.all_gather(mine, ("tensor", "frame"), axis=0, tiled=True)


def gather_columns(shard, frame_count, frame_index):
    part = shard.shape[0] // frame_count
    mine = lax.dynamic_slice_in_dim(shard, frame_index * part, part, 0)
    full = lax.all_gather(mine, ("tensor", "frame"), axis=0, tiled=True)
    return full.reshape(-1, shard.shape[0], shard.shape[1])


def temporal_attention(q, k, v, frame_pos, heads):
    half = HD // 2
    frequency = jnp.exp(-math.log(10000.0) * jnp.arange(half, dtype=jnp.float32) / half)
    angles = frame_pos.astype(jnp.float32)[:, None] * frequency[None, :]
    cosine = jnp.tile(jnp.cos(angles), (1, 2 * heads))[:, None, :]
    sine = jnp.sin(angles)
    sine = jnp.tile(jnp.concatenate([-sine, sine], axis=1), (1, heads))[:, None, :]
    first = (jnp.arange(heads * HD) % HD) < half

    def turn(x):
        x = x.astype(jnp.float32)
        swapped = jnp.where(first, jnp.roll(x, -half, axis=-1), jnp.roll(x, half, axis=-1))
        return (x * cosine + swapped * sine).astype(jnp.bfloat16)

    frames, pp = q.shape[0], q.shape[1]
    q = turn(q).reshape(frames, pp, heads, HD)
    k = turn(k).reshape(frames, pp, heads, HD)
    v = v.reshape(frames, pp, heads, HD)
    scores = jnp.sum(
        q[:, None].astype(jnp.float32) * k[None, :].astype(jnp.float32), axis=-1
    ) * HD ** (-0.5)
    weights = jax.nn.softmax(scores, axis=1).astype(jnp.bfloat16).astype(jnp.float32)
    out = jnp.sum(weights[..., None] * v[None].astype(jnp.float32), axis=1)
    return out.astype(jnp.bfloat16).reshape(frames * pp, heads * HD)


def shards(
    latent, timestep, frame_pos, time_w1, time_w2, ada_w, w_sqkv, w_so, w_tqkv, w_to, w_fc1, w_fc2
):
    frames = lax.axis_size("frame")
    tensors = lax.axis_size("tensor")
    count = frames * tensors
    frame_index = lax.axis_index("frame")
    heads = D // HD
    width = latent.shape[1]
    pp = -(-P_SIZE // (count * 16)) * 16
    padded = count * pp

    time_embed = time_features(timestep, time_w1.shape[0])
    hidden_time = jax.nn.silu(bdot(time_embed, time_w1)).astype(jnp.bfloat16)
    condition = jax.nn.silu(bdot(hidden_time, time_w2)).astype(jnp.bfloat16)
    partial_mod = bdot(condition, ada_w)
    modulation = lax.psum(partial_mod.astype(jnp.bfloat16), "tensor").astype(jnp.float32)[0]

    def mod_vector(index):
        return modulation[index * D : (index + 1) * D]

    def to_patches(block):
        block = jnp.pad(block, ((0, padded - P_SIZE), (0, 0))).reshape(count, pp, width)
        got = lax.all_to_all(block, ("frame", "tensor"), 0, 0, tiled=True)
        got = got.reshape(frames, tensors, pp, width).transpose(0, 2, 1, 3)
        return got.reshape(frames * pp, D)

    def to_features(rows):
        block = rows.reshape(frames, pp, tensors, width).transpose(0, 2, 1, 3)
        got = lax.all_to_all(
            block.reshape(count, pp, width), ("frame", "tensor"), 0, 0, tiled=True
        )
        return got.reshape(padded, width)[:P_SIZE]

    full_rows = lax.all_gather(latent, "tensor", axis=1, tiled=True)
    all_pos = lax.all_gather(frame_pos, "frame", axis=0, tiled=True)
    full_rows, w_so, w_tqkv, w_to, w_fc1, w_fc2 = lax.optimization_barrier(
        (full_rows, w_so, w_tqkv, w_to, w_fc1, w_fc2)
    )
    full_so = gather_rows(w_so, frames, frame_index)
    full_tqkv = gather_columns(w_tqkv, frames, frame_index)
    full_to = gather_rows(w_to, frames, frame_index)
    full_fc1 = gather_columns(w_fc1, frames, frame_index)
    full_fc2 = gather_rows(w_fc2, frames, frame_index)

    residual = to_patches(latent).astype(jnp.float32)
    normed = branch_input(full_rows, mod_vector(0), mod_vector(1))
    attended = to_patches(spatial_attention(normed, w_sqkv))

    stream = (residual + mod_vector(2) * bdot(attended, full_so)).astype(jnp.bfloat16)
    normed = branch_input(stream, mod_vector(3), mod_vector(4))
    qkv = jnp.einsum("rk,tkn->rtn", normed, full_tqkv, preferred_element_type=jnp.float32)
    qkv = qkv.astype(jnp.bfloat16).reshape(frames, pp, heads, 3, HD)
    q, k, v = (qkv[:, :, :, i].reshape(frames, pp, D) for i in range(3))
    attended = temporal_attention(q, k, v, all_pos, heads)
    stream = (stream.astype(jnp.float32) + mod_vector(5) * bdot(attended, full_to)).astype(
        jnp.bfloat16
    )
    normed = branch_input(stream, mod_vector(6), mod_vector(7))
    hidden = jnp.einsum("rk,tkn->rtn", normed, full_fc1, preferred_element_type=jnp.float32)
    hidden = jax.nn.gelu(hidden, approximate=True).astype(jnp.bfloat16)
    hidden = hidden.reshape(frames * pp, -1)
    out = stream.astype(jnp.float32) + mod_vector(8) * bdot(hidden, full_fc2)
    return to_features(out.astype(jnp.bfloat16))


def solution(mesh):
    placed = (
        P("frame", "tensor"),
        P(),
        P("frame"),
        P(),
        P(None, "tensor"),
        P("tensor", None),
        P(None, "tensor"),
        P("tensor", None),
        P(None, "tensor"),
        P("tensor", None),
        P(None, "tensor"),
        P("tensor", None),
    )
    return jax.shard_map(
        shards, mesh=mesh, in_specs=placed, out_specs=P("frame", "tensor"), check_vma=False
    )
```

time: 678 us -> 536 us (0.79)
  waiting for transfers between devices: 455 us -> 262 us
  local copies, waits for them, and re-layouts: 29 us -> 58.3 us
  other arithmetic: 21.7 us -> 34.8 us
  blocking collectives: 79.9 us -> 90.3 us
  starting transfers between devices: 0.46 us -> 7.52 us
    reduce_scatter x3 -> x0, waiting for transfers between devices: 265 us -> none  [shards(): lax.psum_scatter(partial_terms.astype(jnp.bfloat16), 'tensor', scatter_di...]
    all_gather x3 -> x6, waiting for transfers between devices: 189 us -> 244 us  [the longest x2 85.8 us: gather_columns(): full = lax.all_gather(mine, ('tensor', 'frame'), axis=0, tiled=True)]
    all_to_all x0 -> x2, waiting for transfers between devices: none -> 17 us  [to_patches(): got = lax.all_to_all(block, ('frame', 'tensor'), 0, 0, tiled=True)]
    unnamed x24 -> x39, local copies, waits for them, and re-layouts: 1.55 us -> 16.1 us
    psum x1, blocking collectives: 40.3 us -> 54 us  [shards(): lax.psum(partial_mod.astype(jnp.bfloat16), 'tensor').astype(jnp.float32)[0]]
    convert_element_type x3 -> x9, local copies, waits for them, and re-layouts: 0.91 us -> 14.6 us  [the longest x2 6.01 us: shards(): residual = to_patches(latent).astype(jnp.float32)]
    sub x2 -> x1, matrix products: 23.8 us -> 14.5 us  [spatial_attention(): weights = jax.nn.softmax(scores, axis=-1).astype(jnp.bfloat16)]
    all_to_all x2 -> x1, blocking collectives: 39.6 us -> 30.5 us  [to_features(): lax.all_to_all(block.reshape(count, pp, width), ('frame', 'tensor'), 0, 0...]
  transfers between devices with their start and end apart: 6 -> 8, of which waited for: 6 -> 5; matrix products, arithmetic and copies ran while one was open for 1% -> 27% of each run, Pallas kernels for 0% -> 0%
where the time goes in v1:
time: 536 us; the launch traced here: 533 us
  waiting for transfers between devices  262 us (49%)
  blocking collectives  90.3 us (17%)
  matrix products  64.2 us (12%)
  local copies, waits for them, and re-layouts  58.3 us (11%)
  other arithmetic  34.8 us (6%)
  between operations  15.4 us (3%)
  starting transfers between devices  7.52 us (1%)
    all_gather x2, waiting for transfers between devices, gather_columns(): full = lax.all_gather(mine, ('tensor', 'frame'), axis=0, tiled=True)  85.8 us
    all_gather x1, waiting for transfers between devices, shards(): full_rows = lax.all_gather(latent, 'tensor', axis=1, tiled=True)  81.2 us
    all_gather x3, waiting for transfers between devices, gather_rows(): return lax.all_gather(mine, ('tensor', 'frame'), axis=0, tiled=True)  77.3 us
    psum x1, blocking collectives, shards(): lax.psum(partial_mod.astype(jnp.bfloat16), 'tensor').astype(jnp.float32)[0]  54 us
    all_to_all x1, blocking collectives, to_features(): lax.all_to_all(block.reshape(count, pp, width), ('frame', 'tensor'), 0, 0...  30.5 us
    dot_general x7, matrix products, bdot(): return jnp.dot(a, b, preferred_element_type=jnp.float32)  18.1 us
    all_to_all x2, waiting for transfers between devices, to_patches(): got = lax.all_to_all(block, ('frame', 'tensor'), 0, 0, tiled=True)  17 us
    unnamed x39, local copies, waits for them, and re-layouts  16.1 us
  transfers between devices with their start and end apart: 8, of which 5 were waited for; matrix products, arithmetic and copies ran while one was open for 27% of the time, Pallas kernels for 0%

profile of v1, /device:TPU:0, one launch (start us, length us, event | category | flops | bytes accessed | tf_op | source)
XLA Modules:
  0.0 532.6 jit_solution(8553332281090467710)
XLA Ops:
  7.3 81.2 %all-gather.9.cloned.1.call-done = bf16[1920,1152]{0,1:T(8,128)(2,1)} async-done(((bf16[1920,144]{0,1:T(8,128)(2,1)}), bf16[1920,1152]{0,1:T(8,128)(2,1)}) %all-gather.9.cloned.1.call-update) | async-done | bytes 4423696 | tf_op jit(solution)/shard_map/all_gather | solution.py:124
  105.9 3.4 all-to-all-start
  112.2 54.0 %psum.7 = bf16[1,10368]{1,0:T(2,128)(2,1)S(1)} all-reduce(bf16[1,10368]{1,0:T(2,128)(2,1)S(1)} %convert_element_type.193), channel_id=1, replica_groups=mesh['frame'=4,'tensor'=8] {'tensor'}, use_global_device_ids=true, to_apply=%region_0.1 | all-reduce | flops 10368 | bytes 41472 | tf_op jit(solution)/shard_map/psum | solution.py:106
  169.5 3.5 fusion.8
  175.8 14.5 %fusion.77 = (f32[2,1920]{1,0:T(2,128)S(1)}, f32[2,1920,1920]{1,2,0:T(8,128)}) fusion(bf16[1920,2,3,72]{0,3,2,1:T(8,128)(2,1)S(1)} %bitcast.140), kind=kOutput, calls=%fused_computation.136 | convolution fusion | flops 1083803520 | bytes 30612480 | tf_op jit(solution)/shard_map/sub | solution.py:41
  190.3 12.5 %fusion.39 = bf16[2,72,1920]{2,1,0:T(8,128)(2,1)S(1)} fusion(f32[2,1920,1920]{1,2,0:T(8,128)} %get-tuple-element.43, f32[2,1920]{1,0:T(2,128)S(1)} %get-tuple-element.42, bf16[1920,2,3,72]{0,3,2,1:T(8,128)(2,1)} %bitcast.141), kind=kOutput, calls=%fused_computation.44 | convolution fusion | flops 1076705280 | bytes 30612480 | tf_op jit(solution)/shard_map/hpq,qhd->phd/dot_general | solution.py:42
  204.3 3.9 all-to-all-start.1
  210.3 5.8 %all-reduce.2 = s32[4]{0:T(128)S(1)} all-reduce(s32[4]{0:T(128)S(1)} %dynamic-update-slice), channel_id=1, replica_groups=mesh['frame'=4,'tensor'=8] {'frame'}, use_global_device_ids=true, to_apply=%add.2 | all-reduce | flops 4 | bytes 32
  221.7 3.4 reshape.281
  225.1 17.0 %all-to-all-done.1 = bf16[32,64,144]{2,1,0:T(8,128)(2,1)} async-done(((bf16[32,64,144]{2,1,0:T(8,128)(2,1)}), bf16[32,64,144]{2,1,0:T(8,128)(2,1)}, u32[]{:S(2)}, u32[]{:S(2)}) %all-to-all-start.1) | async-done | bytes 589856 | tf_op jit(solution)/shard_map/all_to_all | solution.py:113
  245.8 3.6 reshape.292
  249.4 5.2 reshape.294
  258.5 41.4 %all-gather.11.cloned.1.call-done = bf16[9216,432]{1,0:T(8,128)(2,1)} async-done(((bf16[288,432]{1,0:T(8,128)(2,1)}), bf16[9216,432]{1,0:T(8,128)(2,1)}) %all-gather.11.cloned.1.call-update) | async-done | bytes 7962640 | tf_op jit(solution)/shard_map/all_gather | solution.py:60
  299.9 7.9 %convolution_convert_fusion = bf16[256,8,432]{0,2,1:T(8,128)(2,1)S(1)} fusion(bf16[8,1152,432]{2,1,0:T(8,128)(2,1)} %bitcast.139, f32[256,1152]{1,0:T(8,128)} %copy-done.3, f32[1152]{0:T(1024)S(1)} %get-tuple-element.20, f32[1152]{0:T(1024)S(1)} %get-tuple-element.21, f32[256]{0:T(256)S(1)} %add_rsqrt_fusion.2, f32[256]{0:T(256)S(1)} %broadcast_multiply_fusion.2), kind=kOutput, calls=%fused_computation.56 | convolution fusion | flops 2040791040 | bytes 10923008 | tf_op jit(solution)/shard_map/rk,tkn->rtn/dot_general | solution.py:141
  310.7 3.9 fusion.47
  321.1 7.1 %fusion.44 = (f32[4,64,16,72]{1,0,3,2:T(4,128)}, f32[4,64,16,72]{1,0,3,2:T(4,128)}) fusion(f32[4,64,16,72]{1,0,3,2:T(4,128)S(1)} %bitcast.130, f32[4,64,16,72]{1,0,3,2:T(4,128)S(1)} %bitcast.129, f32[4,72]{0,1:T(8,128)S(1)} %copy.99, f32[4,16,72]{0,2,1:T(8,128)S(1)} %copy-done.7, pred[16,72]{1,0:T(8,128)(4,1)S(1)} %fusion.63, ...), kind=kLoop, calls=%fused_computation.57 | loop fusion | flops 4128768 | bytes 8278272 | tf_op jit(solution)/shard_map/convert_element_type | solution.py:83
  328.2 3.3 copy.100
  333.4 4.7 multiply_reduce_fusion.2
  340.5 4.4 multiply_reduce_fusion.1
  349.2 44.4 %all-gather.13.cloned.1.call-done = bf16[9216,576]{1,0:T(8,128)(2,1)} async-done(((bf16[288,576]{1,0:T(8,128)(2,1)}), bf16[9216,576]{1,0:T(8,128)(2,1)}) %all-gather.13.cloned.1.call-update) | async-done | bytes 10616848 | tf_op jit(solution)/shard_map/all_gather | solution.py:60
  393.7 11.2 %fusion.19 = bf16[256,8,576]{0,2,1:T(8,128)(2,1)} fusion(bf16[8,1152,576]{2,1,0:T(8,128)(2,1)} %bitcast.138, f32[256,1152]{1,0:T(8,128)S(1)} %get-tuple-element.47, f32[1152]{0:T(1024)S(1)} %get-tuple-element.18, f32[1152]{0:T(1024)S(1)} %get-tuple-element.19, f32[256]{0:T(256)S(1)} %add_rsqrt_fusion.1, f32[256]{0:T(256)S(1)} %broadcast_multiply_fusion.1), kind=kOutput, calls=%fused_computation.25 | convolution fusion | flops 2730000384 | bytes 14167040 | tf_op jit(solution)/shard_map/rk,tkn->rtn/dot_general | solution.py:149
  404.9 77.3 %all-gather.15.cloned.1.call-done = bf16[4608,1152]{1,0:T(8,128)(2,1)} async-done(((bf16[144,1152]{1,0:T(8,128)(2,1)}), bf16[4608,1152]{1,0:T(8,128)(2,1)}) %all-gather.15.cloned.1.call-update) | async-done | bytes 10616848 | tf_op jit(solution)/shard_map/all_gather | solution.py:54
  482.1 8.0 %fusion.34 = bf16[256,1152]{1,0:T(8,128)(2,1)S(1)} fusion(f32[256,1152]{1,0:T(8,128)S(1)} %get-tuple-element.47, bf16[256,4608]{0,1:T(8,128)(2,1)} %bitcast.131, bf16[4608,1152]{1,0:T(8,128)(2,1)} %all-gather.15.cloned.1.call-done, f32[1152]{0:T(1024)S(1)} %get-tuple-element.17), kind=kOutput, calls=%fused_computation.39 | convolution fusion | flops 2718793728 | bytes 14750208 | tf_op jit(solution)/shard_map/dot_general | solution.py:31
  491.8 30.5 %all_to_all.15 = bf16[32,64,144]{2,1,0:T(8,128)(2,1)S(1)} all-to-all(bf16[32,64,144]{2,1,0:T(8,128)(2,1)S(1)} %bitcast.134), channel_id=1, replica_groups=mesh['frame'=4,'tensor'=8] {'frame','tensor'}, dimensions={0} | all-to-all | bytes 1179648 | tf_op jit(solution)/shard_map/all_to_all | solution.py:119
  (119 shorter events, 65.2 us)
Async XLA Ops:
  6.5 105.1 %copy-start = (bf16[144,10368]{1,0:T(8,128)(2,1)S(1)}, bf16[144,10368]{1,0:T(8,128)(2,1)}, u32[]{:S(2)}) copy-start(bf16[144,10368]{1,0:T(8,128)(2,1)} %param.17) | copy-start | bytes 8957956
  6.5 82.0 %all-gather.9.cloned.1.call-start = ((), (), s32[]{:S(2)}) async-start(), calls=%async_computation.3 | async-start | bytes 4976640 | tf_op jit(solution)/shard_map/all_gather | solution.py:124
  7.3 238.6 %all-gather.17.cloned.1.call-start = ((), (), s32[]{:S(2)}) async-start(), calls=%async_computation.7 | async-start | bytes 3041280 | tf_op jit(solution)/shard_map/all_gather | solution.py:54
  90.1 159.3 %all-gather.19.cloned.1.call-start = ((), (), s32[]{:S(2)}) async-start(), calls=%async_computation.8 | async-start | bytes 3041280 | tf_op jit(solution)/shard_map/all_gather | solution.py:54
  91.7 208.1 %all-gather.11.cloned.1.call-start = ((), (), s32[]{:S(2)}) async-start(), calls=%async_computation.4 | async-start | bytes 9732096 | tf_op jit(solution)/shard_map/all_gather | solution.py:60
  95.9 6.3 %copy-start.8 = (bf16[1920,144]{0,1:T(8,128)(2,1)S(1)}, bf16[1920,144]{0,1:T(8,128)(2,1)}, u32[]{:S(2)}) copy-start(bf16[1920,144]{0,1:T(8,128)(2,1)} %param.12) | copy-start | bytes 1658884
  95.9 297.8 %all-gather.13.cloned.1.call-start = ((), (), s32[]{:S(2)}) async-start(), calls=%async_computation.5 | async-start | bytes 12165120 | tf_op jit(solution)/shard_map/all_gather | solution.py:60
  100.4 381.8 %all-gather.15.cloned.1.call-start = ((), (), s32[]{:S(2)}) async-start(), calls=%async_computation.6 | async-start | bytes 10948608 | tf_op jit(solution)/shard_map/all_gather | solution.py:54
  103.5 7.8 %copy-start.9 = (bf16[1152,144]{0,1:T(8,128)(2,1)S(1)}, bf16[1152,144]{0,1:T(8,128)(2,1)}, u32[]{:S(2)}) copy-start(bf16[1152,144]{0,1:T(8,128)(2,1)} %param.16) | copy-start | bytes 995332
  105.9 98.4 %all-to-all-start = ((bf16[32,64,144]{2,1,0:T(8,128)(2,1)}), bf16[32,64,144]{2,1,0:T(8,128)(2,1)}, u32[]{:S(2)}, u32[]{:S(2)}) async-start(bf16[32,64,144]{2,1,0:T(8,128)(2,1)} %bitcast.132), calls=%async_computation | async-start | bytes 2097152 | tf_op jit(solution)/shard_map/all_to_all | solution.py:113
  112.2 60.9 %slice-start = ((s8[4423680]{0:T(1024)(128)(4,1)}), s8[229376]{0:T(1024)(128)(4,1)S(1)}, s32[]{:S(2)}) async-start(s8[4423680]{0:T(1024)(128)(4,1)} %bitcast.125), calls=%async_computation.9 | async-start | bytes 458752
  166.4 6.7 %slice-start.1 = ((s8[4423680]{0:T(1024)(128)(4,1)}), s8[4194304]{0:T(1024)(128)(4,1)S(1)}, s32[]{:S(2)}) async-start(s8[4423680]{0:T(1024)(128)(4,1)} %bitcast.125), calls=%async_computation.10 | async-start | bytes 8388608
  169.5 3.6 copy-start.10
  175.8 14.5 %copy-start.11 = (bf16[1920,432]{0,1:T(8,128)(2,1)}, bf16[1920,432]{0,1:T(8,128)(2,1)S(1)}, u32[]{:S(2)}) copy-start(bf16[1920,432]{0,1:T(8,128)(2,1)S(1)} %fusion.28) | copy-start | bytes 4976644
  203.2 5.8 %copy-start.12 = (u32[32]{0:T(128)S(1)}, u32[32]{0:T(128)}, u32[]{:S(2)}) copy-start(u32[32]{0:T(128)} %constant.84) | copy-start | bytes 388
  204.3 37.8 %all-to-all-start.1 = ((bf16[32,64,144]{2,1,0:T(8,128)(2,1)}), bf16[32,64,144]{2,1,0:T(8,128)(2,1)}, u32[]{:S(2)}, u32[]{:S(2)}) async-start(bf16[32,64,144]{2,1,0:T(8,128)(2,1)} %bitcast.11), calls=%async_computation.1 | async-start | bytes 2097152 | tf_op jit(solution)/shard_map/all_to_all | solution.py:113
  257.1 1.1 copy-start.3
  318.9 2.0 copy-start.2
  319.0 2.1 copy-start.7
  328.1 3.3 copy-start.5
  333.4 5.2 copy-start.6
  340.5 5.6 %copy-start.4 = (f32[256,1152]{1,0:T(8,128)S(1)}, f32[256,1152]{1,0:T(8,128)}, u32[]{:S(2)}) copy-start(f32[256,1152]{1,0:T(8,128)} %copy-done.3) | copy-start | bytes 3538948
  491.8 33.8 %copy-start.1 = (bf16[144,10368]{1,0:T(8,128)(2,1)S(1)}, bf16[144,10368]{1,0:T(8,128)(2,1)}, u32[]{:S(2)}) copy-start(bf16[144,10368]{1,0:T(8,128)(2,1)} %param.17) | copy-start | bytes 8957956
Sparse Core Ops, SparseCore 0:
  9.5 78.9 all-gather.8
  91.3 61.2 all-gather.16
  155.5 57.6 all-gather.18
  215.9 83.9 all-gather.10
  302.6 91.0 all-gather.12
  396.4 85.6 all-gather.14

commit v2 on v1

--- a/solution.py
+++ b/solution.py
@@ -3,6 +3,8 @@
 import jax
 import jax.numpy as jnp
 from jax import lax
+from jax.experimental import pallas as pl
+from jax.experimental.pallas import tpu as pltpu
 from jax.sharding import PartitionSpec as P
 
 D = 1152
@@ -31,34 +33,147 @@
     return jnp.dot(a, b, preferred_element_type=jnp.float32)
 
 
-def spatial_attention(normed, w_qkv):
+def ring_place(index, n):
+    odd = index % 2
+    return (1 - odd) * (index // 2) + odd * (n - 1 - index // 2)
+
+
+def ring_member(place, n):
+    back = place // (n // 2)
+    return (1 - back) * (2 * place) + back * (2 * (n - 1 - place) + 1)
+
+
+def exchange_kernel(n, x_ref, part_ref, full_ref, mods_ref, send, recv, msend, mrecv, local):
+    me = lax.axis_index("tensor")
+    place = ring_place(me, n)
+    rows = x_ref.shape[0]
+    half = n // 2
+    cut = max(16, -(-rows // 32) * 16)
+
+    def member(offset):
+        return ring_member(lax.rem(place + offset + 2 * n, n), n)
+
+    barrier = pltpu.get_barrier_semaphore()
+    for k in range(1, n):
+        peer = lax.rem(me + k, n)
+        pl.semaphore_signal(
+            barrier, inc=1, device_id={"tensor": peer}, device_id_type=pl.DeviceIdType.MESH
+        )
+    pl.semaphore_wait(barrier, n - 1)
+
+    def hop(direction, step, lo, size, owner):
+        source = x_ref if step == 0 else full_ref.at[owner]
+        return pltpu.make_async_remote_copy(
+            src_ref=source.at[pl.ds(lo, size)],
+            dst_ref=full_ref.at[owner, pl.ds(lo, size)],
+            send_sem=send.at[direction, step],
+            recv_sem=recv.at[direction, step],
+            device_id={"tensor": member(1 if direction == 0 else -1)},
+            device_id_type=pl.DeviceIdType.MESH,
+        )
+
+    def span(direction, step):
+        if step < half - 1:
+            return 0, rows
+        return (0, cut) if direction == 0 else (cut, rows - cut)
+
+    def outgoing(direction, step):
+        lo, size = span(direction, step)
+        return hop(direction, step, lo, size, member(-step if direction == 0 else step))
+
+    def incoming(direction, step):
+        lo, size = span(direction, step)
+        sign = -1 if direction == 0 else 1
+        return hop(direction, step, lo, size, member(sign * (step + 1)))
+
+    def mod_copy(slot, peer):
+        return pltpu.make_async_remote_copy(
+            src_ref=part_ref,
+            dst_ref=mods_ref.at[slot],
+            send_sem=msend.at[peer],
+            recv_sem=mrecv.at[slot],
+            device_id={"tensor": peer},
+            device_id_type=pl.DeviceIdType.MESH,
+        )
+
+    own = pltpu.make_async_copy(x_ref, full_ref.at[me], local)
+    mods_ref[me] = part_ref[...]
+    for direction in range(2):
+        outgoing(direction, 0).start()
+    for k in range(1, n):
+        mod_copy(me, lax.rem(me + k, n)).start()
+    own.start()
+    for step in range(1, half):
+        for direction in range(2):
+            incoming(direction, step - 1).wait_recv()
+            outgoing(direction, step).start()
+    for direction in range(2):
+        incoming(direction, half - 1).wait_recv()
+    for step in range(half):
+        for direction in range(2):
+            outgoing(direction, step).wait_send()
+    for k in range(1, n):
+        peer = lax.rem(me + k, n)
+        mod_copy(peer, peer).wait_recv()
+        mod_copy(me, peer).wait_send()
+    own.wait()
+
+
+def exchange(n, x_block, part):
+    half = n // 2
+    vmem = pl.BlockSpec(memory_space=pltpu.VMEM)
+    return pl.pallas_call(
+        lambda *refs: exchange_kernel(n, *refs),
+        out_shape=(
+            jax.ShapeDtypeStruct((n,) + x_block.shape, x_block.dtype),
+            jax.ShapeDtypeStruct((n,) + part.shape, part.dtype),
+        ),
+        in_specs=[vmem, vmem],
+        out_specs=(vmem, vmem),
+        scratch_shapes=[
+            pltpu.SemaphoreType.DMA((2, half)),
+            pltpu.SemaphoreType.DMA((2, half)),
+            pltpu.SemaphoreType.DMA((n,)),
+            pltpu.SemaphoreType.DMA((n,)),
+            pltpu.SemaphoreType.DMA,
+        ],
+        compiler_params=pltpu.CompilerParams(
+            collective_id=0, has_side_effects=True, vmem_limit_bytes=24 * 1024 * 1024
+        ),
+        cost_estimate=pl.CostEstimate(flops=0, bytes_accessed=100_000_000, transcendentals=0),
+        name="exchange",
+    )(x_block, part)
+
+
+def spatial_attention(normed_t, w_qkv):
     heads_local = w_qkv.shape[1] // (3 * HD)
-    projected = bdot(normed, w_qkv).astype(jnp.bfloat16)
-    projected = projected.reshape(P_SIZE, heads_local, 3, HD)
+    projected = jnp.einsum(
+        "kn,kp->np", w_qkv, normed_t, preferred_element_type=jnp.float32
+    ).astype(jnp.bfloat16)
+    projected = projected.reshape(heads_local, 3, HD, P_SIZE)
     scores = jnp.einsum(
-        "phd,qhd->hpq", projected[:, :, 0], projected[:, :, 1], preferred_element_type=jnp.float32
+        "hdp,hdq->hpq", projected[:, 0], projected[:, 1], preferred_element_type=jnp.float32
     ) * HD ** (-0.5)
     weights = jax.nn.softmax(scores, axis=-1).astype(jnp.bfloat16)
     attended = jnp.einsum(
-        "hpq,qhd->phd", weights, projected[:, :, 2], preferred_element_type=jnp.float32
+        "hpq,hdq->phd", weights, projected[:, 2], preferred_element_type=jnp.float32
     ).astype(jnp.bfloat16)
     return attended.reshape(P_SIZE, heads_local * HD)
 
 
-def gather_rows(shard, frame_count, frame_index):
-    rows = shard.shape[0]
-    if rows % frame_count:
-        return lax.all_gather(shard, "tensor", axis=0, tiled=True)
-    part = rows // frame_count
-    mine = lax.dynamic_slice_in_dim(shard, frame_index * part, part, 0)
-    return lax.all_gather(mine, ("tensor", "frame"), axis=0, tiled=True)
-
-
-def gather_columns(shard, frame_count, frame_index):
-    part = shard.shape[0] // frame_count
-    mine = lax.dynamic_slice_in_dim(shard, frame_index * part, part, 0)
-    full = lax.all_gather(mine, ("tensor", "frame"), axis=0, tiled=True)
-    return full.reshape(-1, shard.shape[0], shard.shape[1])
+def gather_joined(shard_list, frame_count, frame_index):
+    if any(shard.shape[0] % frame_count for shard in shard_list):
+        return [lax.all_gather(s, "tensor", axis=0, tiled=True) for s in shard_list]
+    mine = []
+    for shard in shard_list:
+        part = shard.shape[0] // frame_count
+        mine.append(lax.dynamic_slice_in_dim(shard, frame_index * part, part, 0))
+    full = lax.all_gather(jnp.concatenate(mine, axis=0), ("tensor", "frame"), axis=0)
+    out, start = [], 0
+    for part in mine:
+        out.append(full[:, start : start + part.shape[0]].reshape(-1, part.shape[1]))
+        start += part.shape[0]
+    return out
 
 
 def temporal_attention(q, k, v, frame_pos, heads):
@@ -102,8 +217,18 @@
     time_embed = time_features(timestep, time_w1.shape[0])
     hidden_time = jax.nn.silu(bdot(time_embed, time_w1)).astype(jnp.bfloat16)
     condition = jax.nn.silu(bdot(hidden_time, time_w2)).astype(jnp.bfloat16)
-    partial_mod = bdot(condition, ada_w)
-    modulation = lax.psum(partial_mod.astype(jnp.bfloat16), "tensor").astype(jnp.float32)[0]
+    partial_mod = bdot(condition, ada_w).reshape(-1, 128)
+    part_rows = partial_mod.shape[0]
+    partial_mod = jnp.pad(partial_mod, ((0, -part_rows % 8), (0, 0)))
+
+    group_one = gather_joined([w_tqkv.T, w_so, w_to], frames, frame_index)
+    full_t, mods = exchange(tensors, latent.T, partial_mod)
+    full_t = full_t.reshape(D, P_SIZE)
+    modulation = jnp.sum(mods, axis=0)[:part_rows].reshape(-1)
+    full_t, w_fc1, w_fc2 = lax.optimization_barrier((full_t, w_fc1, w_fc2))
+    group_two = gather_joined([w_fc1.T, w_fc2], frames, frame_index)
+    full_tqkv, full_so, full_to = group_one
+    full_fc1, full_fc2 = group_two
 
     def mod_vector(index):
         return modulation[index * D : (index + 1) * D]
@@ -121,24 +246,18 @@
         )
         return got.reshape(padded, width)[:P_SIZE]
 
-    full_rows = lax.all_gather(latent, "tensor", axis=1, tiled=True)
     all_pos = lax.all_gather(frame_pos, "frame", axis=0, tiled=True)
-    full_rows, w_so, w_tqkv, w_to, w_fc1, w_fc2 = lax.optimization_barrier(
-        (full_rows, w_so, w_tqkv, w_to, w_fc1, w_fc2)
-    )
-    full_so = gather_rows(w_so, frames, frame_index)
-    full_tqkv = gather_columns(w_tqkv, frames, frame_index)
-    full_to = gather_rows(w_to, frames, frame_index)
-    full_fc1 = gather_columns(w_fc1, frames, frame_index)
-    full_fc2 = gather_rows(w_fc2, frames, frame_index)
-
     residual = to_patches(latent).astype(jnp.float32)
-    normed = branch_input(full_rows, mod_vector(0), mod_vector(1))
-    attended = to_patches(spatial_attention(normed, w_sqkv))
+    rows_t = full_t.astype(jnp.float32)
+    center = rows_t - jnp.mean(rows_t, axis=0, keepdims=True)
+    spread = jnp.mean(center * center, axis=0, keepdims=True)
+    normed_t = center * lax.rsqrt(spread + 1e-06)
+    normed_t = normed_t * (1.0 + mod_vector(1))[:, None] + mod_vector(0)[:, None]
+    attended = to_patches(spatial_attention(normed_t.astype(jnp.bfloat16), w_sqkv))
 
     stream = (residual + mod_vector(2) * bdot(attended, full_so)).astype(jnp.bfloat16)
     normed = branch_input(stream, mod_vector(3), mod_vector(4))
-    qkv = jnp.einsum("rk,tkn->rtn", normed, full_tqkv, preferred_element_type=jnp.float32)
+    qkv = jnp.einsum("rk,nk->rn", normed, full_tqkv, preferred_element_type=jnp.float32)
     qkv = qkv.astype(jnp.bfloat16).reshape(frames, pp, heads, 3, HD)
     q, k, v = (qkv[:, :, :, i].reshape(frames, pp, D) for i in range(3))
     attended = temporal_attention(q, k, v, all_pos, heads)
@@ -146,9 +265,8 @@
         jnp.bfloat16
     )
     normed = branch_input(stream, mod_vector(6), mod_vector(7))
-    hidden = jnp.einsum("rk,tkn->rtn", normed, full_fc1, preferred_element_type=jnp.float32)
+    hidden = jnp.einsum("rk,nk->rn", normed, full_fc1, preferred_element_type=jnp.float32)
     hidden = jax.nn.gelu(hidden, approximate=True).astype(jnp.bfloat16)
-    hidden = hidden.reshape(frames * pp, -1)
     out = stream.astype(jnp.float32) + mod_vector(8) * bdot(hidden, full_fc2)
     return to_features(out.astype(jnp.bfloat16))
 

time: 536 us -> 384 us (0.72)
  waiting for transfers between devices: 262 us -> 36.4 us
  Pallas kernels: 0 us -> 85.7 us
  blocking collectives: 90.3 us -> 36.2 us
  local copies, waits for them, and re-layouts: 58.3 us -> 92.2 us
  starting transfers between devices: 7.52 us -> 17.2 us
    all_gather x6 -> x2, waiting for transfers between devices: 244 us -> 9.43 us  [gather_joined(): lax.all_gather(jnp.concatenate(mine, axis=0), ('tensor', 'frame'), axis=0)]
    pallas_call x0 -> x1, Pallas kernels: none -> 85.7 us  [exchange(): pl.pallas_call(lambda *refs: exchange_kernel(n, *refs), out_shape=(jax.Sh...]
    psum x1 -> x0, blocking collectives: 54 us -> none  [shards(): lax.psum(partial_mod.astype(jnp.bfloat16), 'tensor').astype(jnp.float32)[0]]
    slice x0 -> x3, local copies, waits for them, and re-layouts: none -> 28.3 us  [gather_joined(): out.append(full[:, start:start + part.shape[0]].reshape(-1, part.shape[1]))]
    reshape x0 -> x3, local copies, waits for them, and re-layouts: none -> 13.8 us  [gather_joined(): out.append(full[:, start:start + part.shape[0]].reshape(-1, part.shape[1]))]
    all_to_all x2, waiting for transfers between devices: 17 us -> 26.9 us  [to_patches(): got = lax.all_to_all(block, ('frame', 'tensor'), 0, 0, tiled=True)]
    all_to_all x2, starting transfers between devices: 7.31 us -> 17.1 us  [to_patches(): got = lax.all_to_all(block, ('frame', 'tensor'), 0, 0, tiled=True)]
    unnamed x39 -> x33, local copies, waits for them, and re-layouts: 16.1 us -> 6.76 us
  transfers between devices with their start and end apart: 8 -> 4, of which waited for: 5 -> 3; matrix products, arithmetic and copies ran while one was open for 27% -> 39% of each run, Pallas kernels for 0% -> 23%
where the time goes in v2:
time: 384 us; the launch traced here: 380 us
  local copies, waits for them, and re-layouts  92.2 us (24%)
  Pallas kernels  85.7 us (22%)
  matrix products  61 us (16%)
  waiting for transfers between devices  36.4 us (9%)
  other arithmetic  36.2 us (9%)
  blocking collectives  36.2 us (9%)
  starting transfers between devices  17.2 us (4%)
  between operations  15.4 us (4%)
    pallas_call x1, Pallas kernels, exchange(): pl.pallas_call(lambda *refs: exchange_kernel(n, *refs), out_shape=(jax.Sh...  85.7 us
    all_to_all x1, blocking collectives, to_features(): lax.all_to_all(block.reshape(count, pp, width), ('frame', 'tensor'), 0, 0...  30.2 us
    slice x3, local copies, waits for them, and re-layouts, gather_joined(): out.append(full[:, start:start + part.shape[0]].reshape(-1, part.shape[1]))  28.3 us
    all_to_all x2, waiting for transfers between devices, to_patches(): got = lax.all_to_all(block, ('frame', 'tensor'), 0, 0, tiled=True)  26.9 us
    dot_general x6, matrix products, bdot(): return jnp.dot(a, b, preferred_element_type=jnp.float32)  22.3 us
    all_to_all x2, starting transfers between devices, to_patches(): got = lax.all_to_all(block, ('frame', 'tensor'), 0, 0, tiled=True)  17.1 us
    sub x1, matrix products, spatial_attention(): weights = jax.nn.softmax(scores, axis=-1).astype(jnp.bfloat16)  15.3 us
    reshape x3, local copies, waits for them, and re-layouts, gather_joined(): out.append(full[:, start:start + part.shape[0]].reshape(-1, part.shape[1]))  13.8 us
  transfers between devices with their start and end apart: 4, of which 3 were waited for; matrix products, arithmetic and copies ran while one was open for 39% of the time, Pallas kernels for 23%

profile of v2, /device:TPU:0, one launch (start us, length us, event | category | flops | bytes accessed | tf_op | source)
XLA Modules:
  0.0 380.3 jit_solution(9689921863292044958)
XLA Ops:
  13.5 85.7 %exchange.1 = (bf16[8,144,1920]{2,1,0:T(8,128)(2,1)S(1)}, f32[8,88,128]{2,1,0:T(8,128)S(1)}) custom-call(bf16[144,1920]{1,0:T(8,128)(2,1)S(1)} %bitcast.151, f32[88,128]{1,0:T(8,128)S(1)} %pad.12.refs_1_), custom_call_target="tpu_custom_call" | custom-call | bytes 100000000 | tf_op jit(solution)/shard_map/exchange/pallas_call | solution.py:125
  105.7 12.3 %all-to-all-start = ((bf16[32,64,144]{2,1,0:T(8,128)(2,1)}), bf16[32,64,144]{2,1,0:T(8,128)(2,1)S(1)}, u32[]{:S(2)}, u32[]{:S(2)}) async-start(bf16[32,64,144]{2,1,0:T(8,128)(2,1)} %bitcast), calls=%async_computation | async-start | bytes 2097152 | tf_op jit(solution)/shard_map/all_to_all | solution.py:238
  118.0 3.1 convert_reduce_fusion
  123.1 3.9 %fusion.31 = bf16[1920,432]{0,1:T(8,128)(2,1)} fusion(bf16[1152,432]{0,1:T(8,128)(2,1)S(1)} %copy-done.12, bf16[1152,1920]{1,0:T(8,128)(2,1)S(1)} %bitcast.150, f32[1152]{0:T(1024)S(1)} %get-tuple-element.38, f32[1152]{0:T(1024)S(1)} %get-tuple-element.39, f32[1920]{0:T(1024)S(1)} %add_rsqrt_fusion, f32[1920]{0:T(1024)S(1)} %broadcast_multiply_fusion), kind=kOutput, calls=%fused_computation.36 | convolution fusion | flops 1925130240 | bytes 7102464 | tf_op jit(solution)/shard_map/kn,kp->np/dot_general | solution.py:150
  127.0 15.3 %fusion.92 = (f32[2,1920]{1,0:T(2,128)S(1)}, f32[2,1920,1920]{1,2,0:T(8,128)}) fusion(bf16[2,3,72,1920]{3,2,1,0:T(8,128)(2,1)} %bitcast.170), kind=kOutput, calls=%fused_computation.150 | convolution fusion | flops 1083803520 | bytes 30612480 | tf_op jit(solution)/shard_map/sub | solution.py:157
  142.3 12.3 %fusion.42 = bf16[2,72,1920]{2,1,0:T(8,128)(2,1)S(1)} fusion(f32[2,1920,1920]{1,2,0:T(8,128)} %get-tuple-element.45, f32[2,1920]{1,0:T(2,128)S(1)} %get-tuple-element.44, bf16[2,3,72,1920]{3,2,1,0:T(8,128)(2,1)} %bitcast.171), kind=kOutput, calls=%fused_computation.48 | convolution fusion | flops 1076705280 | bytes 30612480 | tf_op jit(solution)/shard_map/hpq,hdq->phd/dot_general | solution.py:158
  157.8 4.8 %all-to-all-start.1 = ((bf16[32,64,144]{2,1,0:T(8,128)(2,1)}), bf16[32,64,144]{2,1,0:T(8,128)(2,1)}, u32[]{:S(2)}, u32[]{:S(2)}) async-start(bf16[32,64,144]{2,1,0:T(8,128)(2,1)} %bitcast.20), calls=%async_computation.1 | async-start | bytes 2097152 | tf_op jit(solution)/shard_map/all_to_all | solution.py:238
  164.5 6.0 %all-reduce.3 = s32[4]{0:T(128)S(1)} all-reduce(s32[4]{0:T(128)S(1)} %dynamic-update-slice), channel_id=1, replica_groups=mesh['frame'=4,'tensor'=8] {'frame'}, use_global_device_ids=true, to_apply=%add.3 | all-reduce | flops 4 | bytes 32
  179.1 25.3 %all-to-all-done.1 = bf16[32,64,144]{2,1,0:T(8,128)(2,1)} async-done(((bf16[32,64,144]{2,1,0:T(8,128)(2,1)}), bf16[32,64,144]{2,1,0:T(8,128)(2,1)}, u32[]{:S(2)}, u32[]{:S(2)}) %all-to-all-start.1) | async-done | bytes 589856 | tf_op jit(solution)/shard_map/all_to_all | solution.py:238
  208.2 5.8 %fusion.87 = (bf16[32,36,1152]{2,1,0:T(8,128)(2,1)}, bf16[32,36,1152]{2,1,0:T(8,128)(2,1)S(1)}) fusion(bf16[32,180,1152]{2,1,0:T(8,128)(2,1)} %all-gather.8.cloned.1.call-done), kind=kLoop, calls=%fused_computation.145 | loop fusion | bytes 10616832 | tf_op jit(solution)/shard_map/slice | solution.py:174
  216.1 7.2 %slice.153 = bf16[32,108,1152]{2,1,0:T(8,128)(2,1)} slice(bf16[32,180,1152]{2,1,0:T(8,128)(2,1)} %all-gather.8.cloned.1.call-done), slice={[0:32], [0:108], [0:1152]} | slice | bytes 15925248 | tf_op jit(solution)/shard_map/slice | solution.py:174
  223.3 9.4 %reshape.322 = bf16[3456,1152]{1,0:T(8,128)(2,1)} reshape(bf16[32,108,1152]{2,1,0:T(8,128)(2,1)} %slice.153) | data formatting | bytes 15925248 | tf_op jit(solution)/shard_map/reshape | solution.py:174
  236.2 7.1 %convolution_convert_fusion = bf16[256,3456]{1,0:T(8,128)(2,1)} fusion(bf16[3456,1152]{1,0:T(8,128)(2,1)} %reshape.322, f32[256,1152]{1,0:T(8,128)S(1)} %get-tuple-element.47, f32[1152]{0:T(1024)S(1)} %get-tuple-element.35, f32[1152]{0:T(1024)S(1)} %get-tuple-element.36, f32[256]{0:T(256)S(1)} %add_rsqrt_fusion.2, f32[256]{0:T(256)S(1)} %broadcast_multiply_fusion.2), kind=kOutput, calls=%fused_computation.18 | convolution fusion | flops 2040791040 | bytes 10923008 | tf_op jit(solution)/shard_map/rk,nk->rn/dot_general | solution.py:260
  249.3 4.9 %fusion.55 = (f32[4,64,16,1,72]{1,0,4,2,3:T(4,128)}, f32[4,64,16,72]{1,0,3,2:T(4,128)}, f32[4,64,16,1,72]{1,0,4,3,2:T(4,128)S(1)}) fusion(bf16[4,64,16,3,72]{1,0,4,3,2:T(4,128)(2,1)} %reshape.323), kind=kLoop, calls=%fused_computation.70 | loop fusion | flops 884736 | bytes 5308416 | tf_op jit(solution)/shard_map/convert_element_type | solution.py:189
  254.3 3.1 copy.102
  268.5 7.0 %fusion.52 = (f32[4,64,16,72]{1,0,3,2:T(4,128)}, f32[4,64,16,72]{1,0,3,2:T(4,128)}) fusion(f32[4,64,16,72]{1,0,3,2:T(4,128)S(1)} %bitcast.159, f32[4,64,16,72]{1,0,3,2:T(4,128)S(1)} %bitcast.160, f32[4,72]{0,1:T(8,128)S(1)} %copy.97, f32[4,16,72]{0,2,1:T(8,128)S(1)} %copy-done.11, pred[16,72]{1,0:T(8,128)(4,1)S(1)} %fusion.72, ...), kind=kLoop, calls=%fused_computation.64 | loop fusion | flops 4128768 | bytes 8278272 | tf_op jit(solution)/shard_map/convert_element_type | solution.py:198
  275.5 3.2 copy.99
  280.7 4.5 %multiply_reduce_fusion.2 = f32[4,4,64,16]{3,2,1,0:T(8,128)S(1)} fusion(f32[4,64,16,72]{3,2,1,0:T(8,128)} %copy.99, f32[4,64,16,72]{3,2,1,0:T(8,128)} %copy.98), kind=kLoop, calls=%fused_computation.16 | loop fusion | flops 2342912 | bytes 2424832 | tf_op jit(solution)/shard_map/reduce_sum | solution.py:197
  285.7 5.4 %multiply_reduce_fusion.1 = bf16[4,64,16,72]{3,2,1,0:T(8,128)(2,1)} fusion(f32[4,64,16,72]{3,2,1,0:T(8,128)} %copy.102, f32[4,4,64,16]{3,2,1,0:T(8,128)S(1)} %copy.101), kind=kLoop, calls=%fused_computation.15 | loop fusion | flops 2064384 | bytes 1835008 | tf_op jit(solution)/shard_map/reduce_sum | solution.py:201
  296.2 3.3 fusion.94
  299.8 9.4 %all-gather.6.cloned.1.call-done = bf16[9216,1152]{1,0:T(8,128)(2,1)} async-done(((bf16[288,1152]{1,0:T(8,128)(2,1)}), bf16[9216,1152]{1,0:T(8,128)(2,1)}) %all-gather.6.cloned.1.call-update) | async-done | bytes 21233680 | tf_op jit(solution)/shard_map/all_gather | solution.py:171
  309.3 15.3 %fusion.86 = (bf16[32,144,1152]{2,1,0:T(8,128)(2,1)}, bf16[32,144,1152]{2,1,0:T(8,128)(2,1)}) fusion(bf16[32,288,1152]{2,1,0:T(8,128)(2,1)} %bitcast.152), kind=kLoop, calls=%fused_computation.144 | loop fusion | bytes 42467328 | tf_op jit(solution)/shard_map/slice | solution.py:174
  324.6 13.5 %fusion.37 = bf16[256,1152]{1,0:T(8,128)(2,1)S(1)} fusion(f32[256,1152]{1,0:T(8,128)S(1)} %get-tuple-element.49, bf16[4608,1152]{1,0:T(8,128)(2,1)} %bitcast.158, bf16[4608,1152]{1,0:T(8,128)(2,1)} %bitcast.157, f32[1152]{0:T(1024)S(1)} %get-tuple-element.33, f32[1152]{0:T(1024)S(1)} %get-tuple-element.34, f32[256]{0:T(256)S(1)} %add_rsqrt_fusion.1, ...), kind=kOutput, calls=%fused_computation.43 | convolution fusion | flops 5448794112 | bytes 23019008 | tf_op jit(solution)/shard_map/dot_general | solution.py:33
  339.7 30.2 %all_to_all.15 = bf16[32,64,144]{2,1,0:T(8,128)(2,1)S(1)} all-to-all(bf16[32,64,144]{2,1,0:T(8,128)(2,1)S(1)} %bitcast.165), channel_id=1, replica_groups=mesh['frame'=4,'tensor'=8] {'frame','tensor'}, dimensions={0} | all-to-all | bytes 1179648 | tf_op jit(solution)/shard_map/all_to_all | solution.py:244
  (108 shorter events, 66.8 us)
Async XLA Ops:
  6.5 6.4 %copy-start = (bf16[144,10368]{1,0:T(8,128)(2,1)S(1)}, bf16[144,10368]{1,0:T(8,128)(2,1)}, u32[]{:S(2)}) copy-start(bf16[144,10368]{1,0:T(8,128)(2,1)} %param.17) | copy-start | bytes 8957956
  6.5 201.6 %all-gather.8.cloned.1.call-start = ((), (), s32[]{:S(2)}) async-start(), calls=%async_computation.4 | async-start | bytes 13989888 | tf_op jit(solution)/shard_map/all_gather | solution.py:171
  9.5 3.9 %copy-start.4 = (bf16[1920,144]{0,1:T(8,128)(2,1)S(1)}, bf16[1920,144]{0,1:T(8,128)(2,1)}, u32[]{:S(2)}) copy-start(bf16[1920,144]{0,1:T(8,128)(2,1)} %param.12) | copy-start | bytes 1658884
  9.6 299.7 %all-gather.6.cloned.1.call-start = ((), (), s32[]{:S(2)}) async-start(), calls=%async_computation.3 | async-start | bytes 21897216 | tf_op jit(solution)/shard_map/all_gather | solution.py:171
  99.2 2.0 copy-start.2
  105.7 52.1 %all-to-all-start = ((bf16[32,64,144]{2,1,0:T(8,128)(2,1)}), bf16[32,64,144]{2,1,0:T(8,128)(2,1)S(1)}, u32[]{:S(2)}, u32[]{:S(2)}) async-start(bf16[32,64,144]{2,1,0:T(8,128)(2,1)} %bitcast), calls=%async_computation | async-start | bytes 2097152 | tf_op jit(solution)/shard_map/all_to_all | solution.py:238
  118.0 3.8 copy-start.3
  121.1 1.9 copy-start.12
  155.0 8.3 %copy-start.13 = (u32[32]{0:T(128)S(1)}, u32[32]{0:T(128)}, u32[]{:S(2)}) copy-start(u32[32]{0:T(128)} %constant.87) | copy-start | bytes 388
  157.8 14.3 %copy-start.10 = (bf16[32,64,144]{2,1,0:T(8,128)(2,1)}, bf16[32,64,144]{2,1,0:T(8,128)(2,1)S(1)}, u32[]{:S(2)}) copy-start(bf16[32,64,144]{2,1,0:T(8,128)(2,1)S(1)} %all-to-all-done) | copy-start | bytes 1769476
  157.8 46.6 %all-to-all-start.1 = ((bf16[32,64,144]{2,1,0:T(8,128)(2,1)}), bf16[32,64,144]{2,1,0:T(8,128)(2,1)}, u32[]{:S(2)}, u32[]{:S(2)}) async-start(bf16[32,64,144]{2,1,0:T(8,128)(2,1)} %bitcast.20), calls=%async_computation.1 | async-start | bytes 2097152 | tf_op jit(solution)/shard_map/all_to_all | solution.py:238
  223.3 9.4 %copy-start.7 = (bf16[1152,1152]{1,0:T(8,128)(2,1)S(1)}, bf16[1152,1152]{1,0:T(8,128)(2,1)}, u32[]{:S(2)}) copy-start(bf16[1152,1152]{1,0:T(8,128)(2,1)} %reshape.321) | copy-start | bytes 7962628
  235.2 1.0 copy-start.8
  266.4 2.0 copy-start.5
  266.4 2.1 copy-start.11
  275.5 3.2 copy-start.9
  285.7 8.3 %copy-start.6 = (bf16[32,36,1152]{2,1,0:T(8,128)(2,1)S(1)}, bf16[32,36,1152]{2,1,0:T(8,128)(2,1)}, u32[]{:S(2)}) copy-start(bf16[32,36,1152]{2,1,0:T(8,128)(2,1)} %get-tuple-element.17) | copy-start | bytes 7962628
  339.7 33.5 %copy-start.1 = (bf16[144,10368]{1,0:T(8,128)(2,1)S(1)}, bf16[144,10368]{1,0:T(8,128)(2,1)}, u32[]{:S(2)}) copy-start(bf16[144,10368]{1,0:T(8,128)(2,1)} %param.17) | copy-start | bytes 8957956
Sparse Core Ops, SparseCore 0:
  10.2 144.3 all-gather.7
  157.5 151.6 all-gather.5
